TPU v7x, 32 devices: a whole 2x2x4 slice. The times are simulated.
32 devices in a mesh: dp: 8 (over z, x), expert: 4 (over y, core).
Axes of the slice: x: 2, y: 2, z: 4, core: 2. Of those that a mesh axis runs over, the one named last changes fastest.
Arguments:
- layer_in: bfloat16 [8192, 1024], P(('dp', 'expert')), may hold values from -6 to 6
- body_of: int32 [8192], P(('dp', 'expert')), may hold values from 0 to 5, as said below
- expert_of: int32 [8192, 1], P(('dp', 'expert')), may hold values from 0 to 7; in each aligned block of 256 rows (0 to 255, 256 to 511, ...) at most 48 rows name the same one
- w_qkv: bfloat16 [1024, 1536], replicated, may hold values from -0.1875 to 0.1875
- w_o: bfloat16 [1024, 512], replicated, may hold values from -0.25 to 0.25
- w_up: bfloat16 [8, 1024, 1024], P('expert', None, 'dp'), may hold values from -0.1875 to 0.1875
- w_down: bfloat16 [8, 1024, 1024], P('expert', 'dp'), may hold values from -0.1875 to 0.1875
- d_out: bfloat16 [8192, 1024], P(('dp', 'expert')), may hold values from -6 to 6
Outputs:
- out: bfloat16 [8192, 1024], P(('dp', 'expert'))
- grad_input: bfloat16 [8192, 1024], P(('dp', 'expert'))
- grad_qkv: float32 [1024, 1536], P(('dp', 'expert'))
- grad_o: float32 [1024, 512], P(('dp', 'expert'))
- grad_up: float32 [8, 1024, 1024], P('expert', None, 'dp')
- grad_down: float32 [8, 1024, 1024], P('expert', 'dp')
Inputs may be any that keep to these rules, and one draw needn't show every extreme that they name: `body_of`: within each device's 256 rows the ids start at 0 and rise by one at each new body; every body has 16 to 128 tokens, no body crosses a multiple of 128 rows of its device, no block of 128 rows holds more than 3 bodies, and some device holds 3 bodies in each of its blocks. `expert_of`: in the 256 rows of one device no expert is named more than 48 times, a bound that some block reaches.
All inputs are finite; a program needn't handle non-finite values.
Results may differ from a plain program's by a relative error of at most 0.014.
Values may be sent and summed in bfloat16 or wider, within the bound.
A program may use at most 128 MiB of HBM per device.

v0:
```python
import jax
import jax.numpy as jnp
from jax import lax
from jax.sharding import PartitionSpec as P

HD = 64
EPSILON = 1e-06


def rms_norm(values):
    scale = lax.rsqrt(jnp.mean(values * values, axis=-1, keepdims=True) + EPSILON)
    return (values * scale).astype(jnp.bfloat16)


def gelu_tanh(values):
    return jax.nn.gelu(values, approximate=True)


def gelu_back(pre_act, cotangent):
    return jax.vjp(gelu_tanh, pre_act)[1](cotangent)[0]


def row_contract(left, right):
    return lax.dot_general(
        left, right, (((0,), (0,)), ((), ())), preferred_element_type=jnp.float32
    )


def col_contract(left, right):
    return lax.dot_general(
        left, right, (((1,), (1,)), ((), ())), preferred_element_type=jnp.float32
    )


def attention_core(packed, labels_row):
    rows = packed.shape[0]
    blocks = rows // 128
    width = packed.shape[1] // 3
    heads = width // HD
    parts = packed.reshape(blocks, 128, 3, heads, HD)
    query = parts[:, :, 0]
    keys = parts[:, :, 1]
    values = parts[:, :, 2]
    scores = jnp.einsum(
        "bqhc,bkhc->bhqk", query, keys, preferred_element_type=jnp.float32
    ) * HD ** (-0.5)
    labels = labels_row.reshape(blocks, 128)
    same = (labels[:, :, None] == labels[:, None, :])[:, None]
    weights = jnp.where(same, jnp.exp(scores), 0.0)
    probs = (weights / jnp.sum(weights, axis=-1, keepdims=True)).astype(jnp.bfloat16)
    mixed = jnp.einsum("bhqk,bkhc->bqhc", probs, values, preferred_element_type=jnp.float32)
    return mixed.astype(jnp.bfloat16).reshape(rows, width)


def stage_perm(count, bit):
    return [(i, i ^ bit) for i in range(count)]


def halve(values, axis_name, count, axis, bit):
    own = lax.axis_index(axis_name) // bit % 2
    keep = lax.dynamic_index_in_dim(values, own, axis, keepdims=False)
    give = lax.dynamic_index_in_dim(values, 1 - own, axis, keepdims=False).astype(jnp.bfloat16)
    came = lax.ppermute(give, axis_name, stage_perm(count, bit))
    return keep + came.astype(jnp.float32)


def scatter_sum(term):
    groups, shards = (lax.axis_size("dp"), lax.axis_size("expert"))
    rows, cols = term.shape
    own_rows = rows // (groups * shards)
    left = shards
    value = term.reshape(groups * shards * own_rows, cols)
    lead = groups
    bit = 1
    while bit < shards:
        left //= 2
        value = halve(value.reshape(lead, left, 2, own_rows, cols), "expert", shards, 2, bit)
        bit *= 2
    left = groups
    bit = 1
    while bit < groups:
        left //= 2
        value = halve(value.reshape(left, 2, own_rows, cols), "dp", groups, 1, bit)
        bit *= 2
    return value.reshape(own_rows, cols)


def ring_pairs(groups, step):
    half = groups // 2
    return [(i, (i // 2 + step) % half * 2 + i % 2) for i in range(groups)]


def ring_gather(shard, pairs, count):
    slots = [shard]
    for _ in range(count - 1):
        slots.append(lax.ppermute(slots[-1], "dp", pairs))
    return slots


def ring_reduce(slots, pairs):
    count = len(slots)
    total = slots[1 % count]
    for step in range(count - 1):
        came = lax.ppermute(total.astype(jnp.bfloat16), "dp", pairs)
        total = came.astype(jnp.float32) + slots[(step + 2) % count]
    return total


def on_device(layer_in, body_of, expert_of, w_qkv, w_o, w_up, w_down, d_out):
    tok_rows = layer_in.shape[0]
    width = layer_in.shape[1]
    shards = lax.axis_size("expert")
    groups = lax.axis_size("dp")
    half = groups // 2
    local_experts = w_up.shape[0]
    all_experts = local_experts * shards
    capacity = 3 * tok_rows // (2 * all_experts)
    received = shards * capacity
    partner = stage_perm(groups, 1)
    forth, back = (ring_pairs(groups, 1), ring_pairs(groups, -1))
    full_up = jnp.concatenate(ring_gather(w_up, forth, half), axis=2)
    full_down = jnp.concatenate(ring_gather(w_down, forth, half), axis=1)
    ids = expert_of[:, 0]
    at = jnp.arange(tok_rows, dtype=jnp.int32)
    earlier = (ids[:, None] == ids[None, :]) & (at[None, :] < at[:, None])
    ranks = jnp.sum(earlier.astype(jnp.int32), axis=1)
    slots = ids * capacity + ranks
    places = jnp.arange(all_experts * capacity, dtype=jnp.int32)
    spread = (places[:, None] == slots[None, :]).astype(jnp.bfloat16)

    def to_experts(values):
        store = jnp.dot(spread, values, preferred_element_type=jnp.float32).astype(jnp.bfloat16)
        store = store.reshape(shards, local_experts, capacity, width)
        sent = lax.all_to_all(store, "expert", split_axis=0, concat_axis=2, tiled=True)
        own = sent.reshape(local_experts, received, width)
        return jnp.concatenate([own, lax.ppermute(own, "dp", partner)], axis=1)

    def to_tokens(values):
        other = lax.ppermute(values[:, received:].astype(jnp.bfloat16), "dp", partner)
        total = (values[:, :received] + other.astype(jnp.float32)).astype(jnp.bfloat16)
        total = total.reshape(local_experts, shards, capacity, width)
        returned = lax.all_to_all(total, "expert", split_axis=1, concat_axis=0, tiled=True)
        returned = returned.reshape(all_experts * capacity, width)
        return row_contract(spread, returned)

    grads_in = to_experts(d_out)
    layer_f = layer_in.astype(jnp.float32)
    normed, norm_x_back = jax.vjp(rms_norm, layer_f)
    packed = jnp.dot(normed, w_qkv, preferred_element_type=jnp.float32).astype(jnp.bfloat16)
    mixed, core_back = jax.vjp(lambda value: attention_core(value, body_of), packed)
    resid = (layer_f + col_contract(mixed, w_o)).astype(jnp.bfloat16)
    inner, norm_h_back = jax.vjp(rms_norm, resid.astype(jnp.float32))
    inputs = to_experts(inner)
    d_hidden = jnp.einsum("esd,efd->esf", grads_in, full_down, preferred_element_type=jnp.float32)
    pre_act = jnp.einsum("esd,edf->esf", inputs, full_up, preferred_element_type=jnp.float32)
    hidden = gelu_tanh(pre_act).astype(jnp.bfloat16)
    d_pre = gelu_back(pre_act, d_hidden).astype(jnp.bfloat16)
    d_inputs = jnp.einsum("esf,edf->esd", d_pre, full_up, preferred_element_type=jnp.float32)
    d_inner = to_tokens(d_inputs).astype(jnp.bfloat16)
    part_up = jnp.einsum("esd,esf->edf", inputs, d_pre, preferred_element_type=jnp.float32)
    part_down = jnp.einsum("esf,esd->efd", hidden, grads_in, preferred_element_type=jnp.float32)
    grad_up = ring_reduce(jnp.split(part_up, half, axis=2), forth)
    grad_down = ring_reduce(jnp.split(part_down, half, axis=1), forth)
    result = jnp.einsum("esf,efd->esd", hidden, full_down, preferred_element_type=jnp.float32)
    expert_out = to_tokens(result)
    out = (resid.astype(jnp.float32) + expert_out).astype(jnp.bfloat16)
    d_resid = (d_out.astype(jnp.float32) + norm_h_back(d_inner)[0]).astype(jnp.bfloat16)
    grad_o = scatter_sum(row_contract(d_resid, mixed))
    d_mixed = jnp.dot(d_resid, w_o, preferred_element_type=jnp.float32).astype(jnp.bfloat16)
    d_packed = core_back(d_mixed)[0]
    grad_qkv = scatter_sum(row_contract(normed, d_packed))
    d_normed = col_contract(d_packed, w_qkv).astype(jnp.bfloat16)
    grad_input = (d_resid.astype(jnp.float32) + norm_x_back(d_normed)[0]).astype(jnp.bfloat16)
    return (out, grad_input, grad_qkv, grad_o, grad_up, grad_down)


def solution(mesh):
    in_specs = (
        P(("dp", "expert"), None),
        P(("dp", "expert")),
        P(("dp", "expert"), None),
        P(),
        P(),
        P("expert", None, "dp"),
        P("expert", "dp", None),
        P(("dp", "expert"), None),
    )
    out_specs = (
        P(("dp", "expert"), None),
        P(("dp", "expert"), None),
        P(("dp", "expert"), None),
        P(("dp", "expert"), None),
        P("expert", None, "dp"),
        P("expert", "dp", None),
    )
    return jax.shard_map(
        on_device, mesh=mesh, in_specs=in_specs, out_specs=out_specs, check_vma=False
    )
```

profile of v0, /device:TPU:0, one launch (start us, length us, event | category | flops | bytes accessed | tf_op | source)
XLA Modules:
  0.0 248.4 jit_solution(4098963044247727574)
XLA Ops:
  0.6 3.1 %collective-permute-start.1 = (bf16[2,1024,128]{2,1,0:T(8,128)(2,1)}, bf16[2,1024,128]{2,1,0:T(8,128)(2,1)}, u32[]{:S(2)}, u32[]{:S(2)}) collective-permute-start(bf16[2,1024,128]{2,1,0:T(8,128)(2,1)} %param.13), channel_id=1, source_target_pairs={{0,8},{4,12},{8,16},{12,20},{16,24},{20,28},{24,0},{28,4},{1,9},{5... | collective-permute-start | bytes 1572872 | tf_op jit(solution)/shard_map/ppermute | solution.py:96
  3.7 1.6 collective-permute-start.4
  9.0 3.0 %convolution_convert_fusion = bf16[256,1536]{1,0:T(8,128)(2,1)} fusion(bf16[1024,1536]{1,0:T(8,128)(2,1)S(1)} %copy-done, bf16[256,1024]{1,0:T(8,128)(2,1)} %param.8, f32[256]{0:T(256)S(1)} %fusion.71), kind=kOutput, calls=%fused_computation.2 | convolution fusion | flops 806486016 | bytes 4457472 | tf_op jit(solution)/shard_map/dot_general | solution.py:149
  12.0 3.1 %reshape.185 = bf16[2,128,3,8,64]{4,3,2,1,0:T(8,128)(2,1)} reshape(bf16[256,1536]{1,0:T(8,128)(2,1)} %convolution_convert_fusion) | data formatting | bytes 1572864 | tf_op jit(solution)/shard_map/jvp()/reshape | solution.py:40
  15.1 2.5 %fusion.80 = (bf16[2,128,1,8,64]{4,3,2,1,0:T(8,128)(2,1)}, bf16[2,128,1,8,64]{4,3,2,1,0:T(8,128)(2,1)}, bf16[2,128,1,8,64]{4,3,2,1,0:T(8,128)(2,1)}) fusion(bf16[2,128,3,8,64]{4,3,2,1,0:T(8,128)(2,1)} %reshape.185), kind=kLoop, calls=%fused_computation.164 | loop fusion | bytes 1572864 | tf_op jit(solution)/shard_map/jvp()/slice | solution.py:43
  18.9 2.0 copy.91
  21.0 2.0 copy.92
  29.1 4.2 %all-to-all-start = ((bf16[4,2,48,1024]{3,2,1,0:T(8,128)(2,1)}), bf16[4,2,48,1024]{3,2,1,0:T(8,128)(2,1)}, u32[]{:S(2)}, u32[]{:S(2)}) async-start(bf16[4,2,48,1024]{3,2,1,0:T(8,128)(2,1)} %bitcast.159), calls=%async_computation | async-start | bytes 1572864 | tf_op jit(solution)/shard_map/all_to_all | solution.py:134
  33.4 1.6 collective-permute-start.2
  35.1 2.3 convolution_convert_fusion.1
  37.4 7.7 %all-to-all-done = bf16[4,2,48,1024]{3,2,1,0:T(8,128)(2,1)} async-done(((bf16[4,2,48,1024]{3,2,1,0:T(8,128)(2,1)}), bf16[4,2,48,1024]{3,2,1,0:T(8,128)(2,1)}, u32[]{:S(2)}, u32[]{:S(2)}) %all-to-all-start) | async-done | bytes 786464 | tf_op jit(solution)/shard_map/all_to_all | solution.py:134
  45.1 4.2 %all-to-all-start.2 = ((bf16[4,2,48,1024]{3,2,1,0:T(8,128)(2,1)}), bf16[4,2,48,1024]{3,2,1,0:T(8,128)(2,1)}, u32[]{:S(2)}, u32[]{:S(2)}) async-start(bf16[4,2,48,1024]{3,2,1,0:T(8,128)(2,1)} %bitcast.158), calls=%async_computation.2 | async-start | bytes 1572864 | tf_op jit(solution)/shard_map/all_to_all | solution.py:134
  49.3 2.0 constant_dynamic-update-slice_fusion.3
  51.2 2.1 copy.59
  54.8 1.6 collective-permute-start.3
  57.2 4.3 %collective-permute-done.5 = bf16[2,128,1024]{2,1,0:T(8,128)(2,1)} collective-permute-done((bf16[2,128,1024]{2,1,0:T(8,128)(2,1)}, bf16[2,128,1024]{2,1,0:T(8,128)(2,1)}, u32[]{:S(2)}, u32[]{:S(2)}) %collective-permute-start.5) | collective-permute-done | bytes 524320 | tf_op jit(solution)/shard_map/ppermute | solution.py:96
  61.5 1.9 constant_dynamic-update-slice_fusion.2
  63.4 1.9 constant_dynamic-update-slice_fusion.6
  68.1 1.9 constant_dynamic-update-slice_fusion.1
  70.0 1.9 constant_dynamic-update-slice_fusion.5
  72.7 1.9 constant_dynamic-update-slice_fusion
  74.6 8.8 %collective-permute-done.6 = bf16[2,128,1024]{2,1,0:T(8,128)(2,1)} collective-permute-done((bf16[2,128,1024]{2,1,0:T(8,128)(2,1)}, bf16[2,128,1024]{2,1,0:T(8,128)(2,1)}, u32[]{:S(2)}, u32[]{:S(2)}) %collective-permute-start.6) | collective-permute-done | bytes 524320 | tf_op jit(solution)/shard_map/ppermute | solution.py:96
  83.5 1.9 constant_dynamic-update-slice_fusion.4
  85.4 3.0 %fusion.40 = f32[2,384,512]{2,1,0:T(8,128)S(1)} fusion(bf16[2,1024,512]{2,1,0:T(8,128)(2,1)} %constant_dynamic-update-slice_fusion, bf16[2,192,1024]{2,1,0:T(8,128)(2,1)} %collective-permute-done, bf16[2,192,1024]{2,1,0:T(8,128)(2,1)} %bitcast.9), kind=kOutput, calls=%fused_computation.92 | convolution fusion | flops 808452096 | bytes 5242880 | tf_op jit(solution)/shard_map/esd,edf->esf/dot_general | solution.py:155
  88.5 1.8 collective-permute-done.8
  90.3 3.7 %fusion.6 = bf16[2,384,512]{2,1,0:T(8,128)(2,1)S(1)} fusion(f32[2,384,512]{2,1,0:T(8,128)S(1)} %fusion.40, bf16[2,512,1024]{2,1,0:T(8,128)(2,1)} %constant_dynamic-update-slice_fusion.4, bf16[2,192,1024]{2,1,0:T(8,128)(2,1)S(1)} %collective-permute-done.8, bf16[2,192,1024]{2,1,0:T(8,128)(2,1)S(1)} %bitcast.175), kind=kOutput, calls=%fused_computation.21 | convolution fusion | flops 816316416 | bytes 6029312 | tf_op jit(solution)/shard_map/esd,efd->esf/dot_general | solution.py:154
  94.0 2.9 %fusion.81 = f32[2,384,1024]{2,1,0:T(8,128)S(1)} fusion(bf16[2,384,512]{2,1,0:T(8,128)(2,1)S(1)} %fusion.6, bf16[2,1024,512]{2,1,0:T(8,128)(2,1)} %constant_dynamic-update-slice_fusion), kind=kOutput, calls=%fused_computation.165 | convolution fusion | flops 805306368 | bytes 6029312 | tf_op jit(solution)/shard_map/esf,edf->esd/dot_general | solution.py:158
  96.9 1.7 copy-done.3
  101.1 3.3 %fusion.79 = f32[2,384,1024]{2,1,0:T(8,128)S(1)} fusion(bf16[2,512,1024]{2,1,0:T(8,128)(2,1)} %constant_dynamic-update-slice_fusion.4, f32[2,384,512]{2,1,0:T(8,128)} %copy-done.22), kind=kOutput, calls=%fused_computation.163 | convolution fusion | flops 808845312 | bytes 6815744 | tf_op jit(solution)/shard_map/esf,efd->esd/dot_general | solution.py:164
  109.3 1.6 collective-permute-start.23
  110.9 9.4 %collective-permute-done.9 = bf16[2,192,1024]{2,1,0:T(8,128)(2,1)} collective-permute-done((bf16[2,192,1024]{2,1,0:T(8,128)(2,1)}, bf16[2,192,1024]{2,1,0:T(8,128)(2,1)}, u32[]{:S(2)}, u32[]{:S(2)}) %collective-permute-start.9) | collective-permute-done | bytes 786464 | tf_op jit(solution)/shard_map/ppermute | solution.py:139
  122.7 4.2 %all-to-all-start.3 = ((bf16[2,4,48,1024]{3,2,0,1:T(8,128)(2,1)}), bf16[2,4,48,1024]{3,2,0,1:T(8,128)(2,1)}, u32[]{:S(2)}, u32[]{:S(2)}) async-start(bf16[2,4,48,1024]{3,2,0,1:T(8,128)(2,1)} %copy.62), calls=%async_computation.3 | async-start | bytes 1572864 | tf_op jit(solution)/shard_map/all_to_all | solution.py:142
  126.9 2.9 %fusion.39 = f32[2,1024,512]{2,1,0:T(8,128)S(1)} fusion(bf16[2,384,512]{2,1,0:T(8,128)(2,1)} %copy-done.18, bf16[2,192,1024]{2,1,0:T(8,128)(2,1)} %collective-permute-done, bf16[2,192,1024]{2,1,0:T(8,128)(2,1)} %bitcast.9), kind=kOutput, calls=%fused_computation.91 | convolution fusion | flops 808452096 | bytes 6553600 | tf_op jit(solution)/shard_map/esd,esf->edf/dot_general | solution.py:160
  129.8 2.0 copy-done.2
  132.9 1.6 collective-permute-start.20
  134.5 2.3 fusion.34
  136.9 1.8 all-to-all-done.3
  138.7 2.0 fusion.32
  143.0 1.8 copy.63
  144.8 1.7 reshape.175
  146.5 1.7 fusion.14
  148.1 1.7 fusion.22
  155.0 2.0 copy.70
  157.0 2.3 fusion.42
  159.3 2.7 %copy-done.1 = f32[8,2,2,32,1536]{4,3,2,1,0:T(8,128)} copy-done((f32[8,2,2,32,1536]{4,3,2,1,0:T(8,128)}, f32[8,2,2,32,1536]{4,3,2,1,0:T(8,128)S(1)}, u32[]{:S(2)}) %copy-start.1) | copy-done | bytes 6291480
  163.4 2.5 fusion.36
  165.9 1.6 collective-permute-start.21
  169.8 4.2 %all-to-all-start.1 = ((bf16[2,4,48,1024]{3,2,0,1:T(8,128)(2,1)}), bf16[2,4,48,1024]{3,2,0,1:T(8,128)(2,1)}, u32[]{:S(2)}, u32[]{:S(2)}) async-start(bf16[2,4,48,1024]{3,2,0,1:T(8,128)(2,1)} %copy.60), calls=%async_computation.1 | async-start | bytes 1572864 | tf_op jit(solution)/shard_map/all_to_all | solution.py:142
  174.0 2.3 fusion.33
  176.4 6.3 %collective-permute-done.21 = bf16[2,1024,128]{2,1,0:T(8,128)(2,1)} collective-permute-done((bf16[2,1024,128]{2,1,0:T(8,128)(2,1)}, bf16[2,1024,128]{2,1,0:T(8,128)(2,1)}, u32[]{:S(2)}, u32[]{:S(2)}) %collective-permute-start.21) | collective-permute-done | bytes 524320 | tf_op jit(solution)/shard_map/ppermute | solution.py:104
  182.7 2.3 fusion.35
  185.0 2.1 copy.73
  190.8 2.6 %fusion.11 = bf16[256,1024]{1,0:T(8,128)(2,1)} fusion(bf16[384,1024]{1,0:T(8,128)(2,1)} %bitcast.13, bf16[256,1024]{1,0:T(8,128)(2,1)} %copy-done.7, s32[256]{0:T(256)S(1)} %multiply_add_fusion.1), kind=kOutput, calls=%fused_computation.45 | convolution fusion | flops 202211328 | bytes 1836032 | tf_op jit(solution)/shard_map/dot_general | solution.py:24
  193.4 3.0 %bitcast_add_fusion = f32[8,2,32,1536]{3,2,1,0:T(8,128)S(1)} fusion(bf16[8,2,32,1536]{3,2,1,0:T(8,128)(2,1)} %collective-permute-done.10, f32[8,2,2,32,1536]{4,3,2,1,0:T(8,128)} %copy-done.1, s32[]{:T(128)S(6)} %select_n.111), kind=kLoop, calls=%fused_computation | loop fusion | flops 1572864 | bytes 7864324 | tf_op jit(solution)/shard_map/add | solution.py:64
  198.0 1.9 collective-permute-start.16
  199.9 2.5 %slice_add_fusion.2 = f32[2,128,1024]{2,1,0:T(8,128)} fusion(f32[2,512,1024]{2,1,0:T(8,128)} %copy-done.16, bf16[2,128,1024]{2,1,0:T(8,128)(2,1)} %collective-permute-done.25), kind=kLoop, calls=%fused_computation.74 | loop fusion | flops 524288 | bytes 2621440 | tf_op jit(solution)/shard_map/add | solution.py:105
  202.4 19.7 %collective-permute-done.16 = bf16[8,1,32,512]{3,2,1,0:T(8,128)(2,1)S(1)} collective-permute-done((bf16[8,1,32,512]{3,2,1,0:T(8,128)(2,1)S(1)}, bf16[8,1,32,512]{3,2,1,0:T(8,128)(2,1)S(1)}, u32[]{:S(2)}, u32[]{:S(2)}) %collective-permute-start.16) | collective-permute-done | bytes 262176 | tf_op jit(solution)/shard_map/ppermute | solution.py:63
  222.2 1.6 collective-permute-start.17
  224.7 2.4 slice_add_fusion.5
  227.1 1.6 collective-permute-done.17
  228.8 7.0 %collective-permute-done.12 = bf16[4,32,1536]{2,1,0:T(8,128)(2,1)S(1)} collective-permute-done((bf16[4,32,1536]{2,1,0:T(8,128)(2,1)S(1)}, bf16[4,32,1536]{2,1,0:T(8,128)(2,1)S(1)}, u32[]{:S(2)}, u32[]{:S(2)}) %collective-permute-start.12) | collective-permute-done | bytes 393248 | tf_op jit(solution)/shard_map/ppermute | solution.py:63
  236.1 4.4 %collective-permute-start.19 = (bf16[1,32,512]{2,1,0:T(8,128)(2,1)S(1)}, bf16[1,32,512]{2,1,0:T(8,128)(2,1)S(1)}, u32[]{:S(2)}, u32[]{:S(2)}) collective-permute-start(bf16[1,32,512]{2,1,0:T(8,128)(2,1)S(1)} %dynamic-slice_convert_fusion.7), channel_id=1, source_target_pairs={{0,16},{4,20},{8,24},{12,28},{16,0},{20,4},{24,8},{28,12},{1,17},{... | collective-permute-start | bytes 98312 | tf_op jit(solution)/shard_map/ppermute | solution.py:63
  242.2 2.7 %collective-permute-start.14 = (bf16[1,32,1536]{2,1,0:T(8,128)(2,1)S(1)}, bf16[1,32,1536]{2,1,0:T(8,128)(2,1)S(1)}, u32[]{:S(2)}, u32[]{:S(2)}) collective-permute-start(bf16[1,32,1536]{2,1,0:T(8,128)(2,1)S(1)} %dynamic-slice_convert_fusion.5), channel_id=1, source_target_pairs={{0,16},{4,20},{8,24},{12,28},{16,0},{20,4},{24,8},{28,12},{1,17},{... | collective-permute-start | bytes 294920 | tf_op jit(solution)/shard_map/ppermute | solution.py:63
  245.5 2.2 collective-permute-done.14
  (157 shorter events, 48.7 us)
Async XLA Ops:
  0.6 8.4 %copy-start = (bf16[1024,1536]{1,0:T(8,128)(2,1)S(1)}, bf16[1024,1536]{1,0:T(8,128)(2,1)}, u32[]{:S(2)}) copy-start(bf16[1024,1536]{1,0:T(8,128)(2,1)} %param.11) | copy-start | bytes 9437188
  0.6 32.7 %collective-permute-start.1 = (bf16[2,1024,128]{2,1,0:T(8,128)(2,1)}, bf16[2,1024,128]{2,1,0:T(8,128)(2,1)}, u32[]{:S(2)}, u32[]{:S(2)}) collective-permute-start(bf16[2,1024,128]{2,1,0:T(8,128)(2,1)} %param.13), channel_id=1, source_target_pairs={{0,8},{4,12},{8,16},{12,20},{16,24},{20,28},{24,0},{28,4},{1,9},{5... | collective-permute-start | bytes 1572872 | tf_op jit(solution)/shard_map/ppermute | solution.py:96
  3.7 31.3 %collective-permute-start.4 = (bf16[2,128,1024]{2,1,0:T(8,128)(2,1)}, bf16[2,128,1024]{2,1,0:T(8,128)(2,1)}, u32[]{:S(2)}, u32[]{:S(2)}) collective-permute-start(bf16[2,128,1024]{2,1,0:T(8,128)(2,1)} %param.14), channel_id=1, source_target_pairs={{0,8},{4,12},{8,16},{12,20},{16,24},{20,28},{24,0},{28,4},{1,9},{5... | collective-permute-start | bytes 1572872 | tf_op jit(solution)/shard_map/ppermute | solution.py:96
  24.4 1.0 copy-start.14
  24.5 1.4 copy-start.20
  24.5 1.9 copy-start.24
  24.6 1.0 copy-start.13
  25.6 3.5 %copy-start.26 = (bf16[2,128,8,64]{1,0,3,2:T(2,128)(2,1)}, bf16[2,128,8,64]{1,0,3,2:T(2,128)(2,1)S(1)}, u32[]{:S(2)}) copy-start(bf16[2,128,8,64]{1,0,3,2:T(2,128)(2,1)S(1)} %copy.58) | copy-start | bytes 786436
  27.0 0.8 copy-start.7
  29.1 15.9 %all-to-all-start = ((bf16[4,2,48,1024]{3,2,1,0:T(8,128)(2,1)}), bf16[4,2,48,1024]{3,2,1,0:T(8,128)(2,1)}, u32[]{:S(2)}, u32[]{:S(2)}) async-start(bf16[4,2,48,1024]{3,2,1,0:T(8,128)(2,1)} %bitcast.159), calls=%async_computation | async-start | bytes 1572864 | tf_op jit(solution)/shard_map/all_to_all | solution.py:134
  33.4 21.4 %collective-permute-start.2 = (bf16[2,1024,128]{2,1,0:T(8,128)(2,1)}, bf16[2,1024,128]{2,1,0:T(8,128)(2,1)}, u32[]{:S(2)}, u32[]{:S(2)}) collective-permute-start(bf16[2,1024,128]{2,1,0:T(8,128)(2,1)} %collective-permute-done.1), channel_id=1, source_target_pairs={{0,8},{4,12},{8,16},{12,20},{16,24},{20,28},{24,0},{28,4},{1,9},{5... | collective-permute-start | bytes 1572872 | tf_op jit(solution)/shard_map/ppermute | solution.py:96
  35.0 26.5 %collective-permute-start.5 = (bf16[2,128,1024]{2,1,0:T(8,128)(2,1)}, bf16[2,128,1024]{2,1,0:T(8,128)(2,1)}, u32[]{:S(2)}, u32[]{:S(2)}) collective-permute-start(bf16[2,128,1024]{2,1,0:T(8,128)(2,1)} %collective-permute-done.4), channel_id=1, source_target_pairs={{0,8},{4,12},{8,16},{12,20},{16,24},{20,28},{24,0},{28,4},{1,9},{5... | collective-permute-start | bytes 1572872 | tf_op jit(solution)/shard_map/ppermute | solution.py:96
  45.1 20.2 %all-to-all-start.2 = ((bf16[4,2,48,1024]{3,2,1,0:T(8,128)(2,1)}), bf16[4,2,48,1024]{3,2,1,0:T(8,128)(2,1)}, u32[]{:S(2)}, u32[]{:S(2)}) async-start(bf16[4,2,48,1024]{3,2,1,0:T(8,128)(2,1)} %bitcast.158), calls=%async_computation.2 | async-start | bytes 1572864 | tf_op jit(solution)/shard_map/all_to_all | solution.py:134
  49.3 7.1 %copy-start.30 = (bf16[2,128,1024]{2,1,0:T(8,128)(2,1)S(1)}, bf16[2,128,1024]{2,1,0:T(8,128)(2,1)}, u32[]{:S(2)}) copy-start(bf16[2,128,1024]{2,1,0:T(8,128)(2,1)} %param.14) | copy-start | bytes 1572868
  53.3 32.1 %collective-permute-start = (bf16[2,192,1024]{2,1,0:T(8,128)(2,1)}, bf16[2,192,1024]{2,1,0:T(8,128)(2,1)}, u32[]{:S(2)}, u32[]{:S(2)}) collective-permute-start(bf16[2,192,1024]{2,1,0:T(8,128)(2,1)} %bitcast.9), channel_id=1, source_target_pairs={{0,4},{4,0},{8,12},{12,8},{16,20},{20,16},{24,28},{28,24},{1,5},{5... | collective-permute-start | bytes 2359304 | tf_op jit(solution)/shard_map/ppermute | solution.py:136
  54.8 17.9 %collective-permute-start.3 = (bf16[2,1024,128]{2,1,0:T(8,128)(2,1)}, bf16[2,1024,128]{2,1,0:T(8,128)(2,1)}, u32[]{:S(2)}, u32[]{:S(2)}) collective-permute-start(bf16[2,1024,128]{2,1,0:T(8,128)(2,1)} %collective-permute-done.2), channel_id=1, source_target_pairs={{0,8},{4,12},{8,16},{12,20},{16,24},{20,28},{24,0},{28,4},{1,9},{5... | collective-permute-start | bytes 1572872 | tf_op jit(solution)/shard_map/ppermute | solution.py:96
  61.5 22.0 %collective-permute-start.6 = (bf16[2,128,1024]{2,1,0:T(8,128)(2,1)}, bf16[2,128,1024]{2,1,0:T(8,128)(2,1)}, u32[]{:S(2)}, u32[]{:S(2)}) collective-permute-start(bf16[2,128,1024]{2,1,0:T(8,128)(2,1)} %collective-permute-done.5), channel_id=1, source_target_pairs={{0,8},{4,12},{8,16},{12,20},{16,24},{20,28},{24,0},{28,4},{1,9},{5... | collective-permute-start | bytes 1572872 | tf_op jit(solution)/shard_map/ppermute | solution.py:96
  66.5 23.8 %copy-start.28 = (bf16[1,2,4,48,1024]{4,3,2,1,0:T(8,128)(2,1)}, bf16[1,2,4,48,1024]{4,3,2,1,0:T(8,128)(2,1)S(1)}, u32[]{:S(2)}) copy-start(bf16[1,2,4,48,1024]{4,3,2,1,0:T(8,128)(2,1)S(1)} %copy.61) | copy-start | bytes 2359300
  66.5 23.7 %collective-permute-start.8 = (bf16[2,192,1024]{2,1,0:T(8,128)(2,1)S(1)}, bf16[2,192,1024]{2,1,0:T(8,128)(2,1)S(1)}, u32[]{:S(2)}, u32[]{:S(2)}) collective-permute-start(bf16[2,192,1024]{2,1,0:T(8,128)(2,1)S(1)} %bitcast.174), channel_id=1, source_target_pairs={{0,4},{4,0},{8,12},{12,8},{16,20},{20,16},{24,28},{28,24},{1,5},{5... | collective-permute-start | bytes 2359304 | tf_op jit(solution)/shard_map/ppermute | solution.py:136
  88.4 5.5 %copy-start.22 = (f32[2,384,512]{2,1,0:T(8,128)}, f32[2,384,512]{2,1,0:T(8,128)S(1)}, u32[]{:S(2)}) copy-start(f32[2,384,512]{2,1,0:T(8,128)S(1)} %fusion.40) | copy-start | bytes 4718596
  90.3 3.7 %copy-start.33 = (bf16[2,192,1024]{2,1,0:T(8,128)(2,1)}, bf16[2,192,1024]{2,1,0:T(8,128)(2,1)S(1)}, u32[]{:S(2)}) copy-start(bf16[2,192,1024]{2,1,0:T(8,128)(2,1)S(1)} %collective-permute-done.8) | copy-start | bytes 2359300
  93.9 2.9 %copy-start.18 = (bf16[2,384,512]{2,1,0:T(8,128)(2,1)}, bf16[2,384,512]{2,1,0:T(8,128)(2,1)S(1)}, u32[]{:S(2)}) copy-start(bf16[2,384,512]{2,1,0:T(8,128)(2,1)S(1)} %fusion.6) | copy-start | bytes 2359300
  96.8 1.7 copy-start.3
  99.6 20.8 %collective-permute-start.9 = (bf16[2,192,1024]{2,1,0:T(8,128)(2,1)}, bf16[2,192,1024]{2,1,0:T(8,128)(2,1)}, u32[]{:S(2)}, u32[]{:S(2)}) collective-permute-start(bf16[2,192,1024]{2,1,0:T(8,128)(2,1)} %slice.45), channel_id=1, source_target_pairs={{0,4},{4,0},{8,12},{12,8},{16,20},{20,16},{24,28},{28,24},{1,5},{5... | collective-permute-start | bytes 2359304 | tf_op jit(solution)/shard_map/ppermute | solution.py:139
  101.1 5.7 %copy-start.29 = (bf16[1,2,4,48,1024]{4,3,2,1,0:T(8,128)(2,1)S(1)}, bf16[1,2,4,48,1024]{4,3,2,1,0:T(8,128)(2,1)}, u32[]{:S(2)}) copy-start(bf16[1,2,4,48,1024]{4,3,2,1,0:T(8,128)(2,1)} %copy-done.28) | copy-start | bytes 2359300
  101.1 5.7 %copy-start.34 = (bf16[2,192,1024]{2,1,0:T(8,128)(2,1)S(1)}, bf16[2,192,1024]{2,1,0:T(8,128)(2,1)}, u32[]{:S(2)}) copy-start(bf16[2,192,1024]{2,1,0:T(8,128)(2,1)} %copy-done.33) | copy-start | bytes 2359300
  104.4 1.9 copy-start.5
  104.4 2.6 %copy-start.23 = (f32[2,384,512]{2,1,0:T(8,128)S(1)}, f32[2,384,512]{2,1,0:T(8,128)}, u32[]{:S(2)}) copy-start(f32[2,384,512]{2,1,0:T(8,128)} %copy-done.22) | copy-start | bytes 4718596
  106.3 61.2 %collective-permute-start.7 = (bf16[2,192,1024]{2,1,0:T(8,128)(2,1)}, bf16[2,192,1024]{2,1,0:T(8,128)(2,1)}, u32[]{:S(2)}, u32[]{:S(2)}) collective-permute-start(bf16[2,192,1024]{2,1,0:T(8,128)(2,1)} %slice.46), channel_id=1, source_target_pairs={{0,4},{4,0},{8,12},{12,8},{16,20},{20,16},{24,28},{28,24},{1,5},{5... | collective-permute-start | bytes 2359304 | tf_op jit(solution)/shard_map/ppermute | solution.py:139
  106.9 13.4 %copy-start.4 = (f32[2,384,1024]{2,1,0:T(8,128)S(1)}, f32[2,384,1024]{2,1,0:T(8,128)}, u32[]{:S(2)}) copy-start(f32[2,384,1024]{2,1,0:T(8,128)} %copy-done.3) | copy-start | bytes 9437188
  108.3 13.4 %copy-start.16 = (f32[2,512,1024]{2,1,0:T(8,128)}, f32[2,512,1024]{2,1,0:T(8,128)S(1)}, u32[]{:S(2)}) copy-start(f32[2,512,1024]{2,1,0:T(8,128)S(1)} %fusion.37) | copy-start | bytes 12582916
  109.3 25.1 %collective-permute-start.23 = (bf16[2,128,1024]{2,1,0:T(8,128)(2,1)}, bf16[2,128,1024]{2,1,0:T(8,128)(2,1)}, u32[]{:S(2)}, u32[]{:S(2)}) collective-permute-start(bf16[2,128,1024]{2,1,0:T(8,128)(2,1)} %split.58), channel_id=1, source_target_pairs={{0,8},{4,12},{8,16},{12,20},{16,24},{20,28},{24,0},{28,4},{1,9},{5... | collective-permute-start | bytes 1572872 | tf_op jit(solution)/shard_map/ppermute | solution.py:104
  122.7 15.9 %all-to-all-start.3 = ((bf16[2,4,48,1024]{3,2,0,1:T(8,128)(2,1)}), bf16[2,4,48,1024]{3,2,0,1:T(8,128)(2,1)}, u32[]{:S(2)}, u32[]{:S(2)}) async-start(bf16[2,4,48,1024]{3,2,0,1:T(8,128)(2,1)} %copy.62), calls=%async_computation.3 | async-start | bytes 1572864 | tf_op jit(solution)/shard_map/all_to_all | solution.py:142
  129.8 2.0 copy-start.2
  132.9 30.5 %collective-permute-start.20 = (bf16[2,1024,128]{2,1,0:T(8,128)(2,1)}, bf16[2,1024,128]{2,1,0:T(8,128)(2,1)}, u32[]{:S(2)}, u32[]{:S(2)}) collective-permute-start(bf16[2,1024,128]{2,1,0:T(8,128)(2,1)} %split.59), channel_id=1, source_target_pairs={{0,8},{4,12},{8,16},{12,20},{16,24},{20,28},{24,0},{28,4},{1,9},{5... | collective-permute-start | bytes 1572872 | tf_op jit(solution)/shard_map/ppermute | solution.py:104
  136.8 37.3 %collective-permute-start.24 = (bf16[2,128,1024]{2,1,0:T(8,128)(2,1)}, bf16[2,128,1024]{2,1,0:T(8,128)(2,1)}, u32[]{:S(2)}, u32[]{:S(2)}) collective-permute-start(bf16[2,128,1024]{2,1,0:T(8,128)(2,1)} %fusion.34), channel_id=1, source_target_pairs={{0,8},{4,12},{8,16},{12,20},{16,24},{20,28},{24,0},{28,4},{1,9},{5... | collective-permute-start | bytes 1572872 | tf_op jit(solution)/shard_map/ppermute | solution.py:104
  138.6 2.0 copy-start.8
  138.6 2.0 copy-start.19
  138.7 3.2 %copy-start.25 = (bf16[1024,512]{1,0:T(8,128)(2,1)S(1)}, bf16[1024,512]{1,0:T(8,128)(2,1)}, u32[]{:S(2)}) copy-start(bf16[1024,512]{1,0:T(8,128)(2,1)} %param.12) | copy-start | bytes 3145732
  146.5 3.4 %copy-start.15 = (f32[2,8,128,128]{2,3,1,0:T(8,128)S(1)}, f32[2,8,128,128]{2,3,1,0:T(8,128)}, u32[]{:S(2)}) copy-start(f32[2,8,128,128]{2,3,1,0:T(8,128)} %copy-done.14) | copy-start | bytes 3145732
  146.5 3.4 %copy-start.32 = (bf16[2,128,1,8,64]{1,4,3,0,2:T(8,128)(2,1)S(1)}, bf16[2,128,1,8,64]{1,4,3,0,2:T(8,128)(2,1)}, u32[]{:S(2)}) copy-start(bf16[2,128,1,8,64]{1,4,3,0,2:T(8,128)(2,1)} %copy.92) | copy-start | bytes 786436
  149.9 1.0 copy-start.31
  151.3 1.1 copy-start.21
  152.3 1.3 copy-start.17
  152.4 1.2 copy-start.10
  159.3 2.7 %copy-start.1 = (f32[8,2,2,32,1536]{4,3,2,1,0:T(8,128)}, f32[8,2,2,32,1536]{4,3,2,1,0:T(8,128)S(1)}, u32[]{:S(2)}) copy-start(f32[8,2,2,32,1536]{4,3,2,1,0:T(8,128)S(1)} %fusion.42) | copy-start | bytes 18874372
  162.0 5.4 %copy-start.6 = (f32[2,384,1024]{2,1,0:T(8,128)S(1)}, f32[2,384,1024]{2,1,0:T(8,128)}, u32[]{:S(2)}) copy-start(f32[2,384,1024]{2,1,0:T(8,128)} %copy-done.5) | copy-start | bytes 9437188
  163.4 30.0 %collective-permute-start.10 = (bf16[8,2,32,1536]{3,2,1,0:T(8,128)(2,1)}, bf16[8,2,32,1536]{3,2,1,0:T(8,128)(2,1)}, u32[]{:S(2)}, u32[]{:S(2)}) collective-permute-start(bf16[8,2,32,1536]{3,2,1,0:T(8,128)(2,1)} %fusion.7), channel_id=1, source_target_pairs={{0,1},{1,0},{2,3},{3,2},{4,5},{5,4},{6,7},{7,6},{8,9},{9,8},{10,11... | collective-permute-start | bytes 4718600 | tf_op jit(solution)/shard_map/ppermute | solution.py:63
  165.9 16.9 %collective-permute-start.21 = (bf16[2,1024,128]{2,1,0:T(8,128)(2,1)}, bf16[2,1024,128]{2,1,0:T(8,128)(2,1)}, u32[]{:S(2)}, u32[]{:S(2)}) collective-permute-start(bf16[2,1024,128]{2,1,0:T(8,128)(2,1)} %fusion.36), channel_id=1, source_target_pairs={{0,8},{4,12},{8,16},{12,20},{16,24},{20,28},{24,0},{28,4},{1,9},{5... | collective-permute-start | bytes 1572872 | tf_op jit(solution)/shard_map/ppermute | solution.py:104
  169.8 21.0 %all-to-all-start.1 = ((bf16[2,4,48,1024]{3,2,0,1:T(8,128)(2,1)}), bf16[2,4,48,1024]{3,2,0,1:T(8,128)(2,1)}, u32[]{:S(2)}, u32[]{:S(2)}) async-start(bf16[2,4,48,1024]{3,2,0,1:T(8,128)(2,1)} %copy.60), calls=%async_computation.1 | async-start | bytes 1572864 | tf_op jit(solution)/shard_map/all_to_all | solution.py:142
  176.3 10.8 %copy-start.27 = (bf16[2,128,8,64]{1,0,3,2:T(2,128)(2,1)S(1)}, bf16[2,128,8,64]{1,0,3,2:T(2,128)(2,1)}, u32[]{:S(2)}) copy-start(bf16[2,128,8,64]{1,0,3,2:T(2,128)(2,1)} %copy-done.26) | copy-start | bytes 786436
  176.3 23.6 %collective-permute-start.25 = (bf16[2,128,1024]{2,1,0:T(8,128)(2,1)}, bf16[2,128,1024]{2,1,0:T(8,128)(2,1)}, u32[]{:S(2)}, u32[]{:S(2)}) collective-permute-start(bf16[2,128,1024]{2,1,0:T(8,128)(2,1)} %fusion.33), channel_id=1, source_target_pairs={{0,8},{4,12},{8,16},{12,20},{16,24},{20,28},{24,0},{28,4},{1,9},{5... | collective-permute-start | bytes 1572872 | tf_op jit(solution)/shard_map/ppermute | solution.py:104
  185.0 39.6 %collective-permute-start.22 = (bf16[2,1024,128]{2,1,0:T(8,128)(2,1)}, bf16[2,1024,128]{2,1,0:T(8,128)(2,1)}, u32[]{:S(2)}, u32[]{:S(2)}) collective-permute-start(bf16[2,1024,128]{2,1,0:T(8,128)(2,1)} %fusion.35), channel_id=1, source_target_pairs={{0,8},{4,12},{8,16},{12,20},{16,24},{20,28},{24,0},{28,4},{1,9},{5... | collective-permute-start | bytes 1572872 | tf_op jit(solution)/shard_map/ppermute | solution.py:104
  188.6 1.3 copy-start.11
  190.8 5.9 %collective-permute-start.15 = (bf16[8,2,32,512]{3,2,1,0:T(8,128)(2,1)}, bf16[8,2,32,512]{3,2,1,0:T(8,128)(2,1)}, u32[]{:S(2)}, u32[]{:S(2)}) collective-permute-start(bf16[8,2,32,512]{3,2,1,0:T(8,128)(2,1)} %fusion.45), channel_id=1, source_target_pairs={{0,1},{1,0},{2,3},{3,2},{4,5},{5,4},{6,7},{7,6},{8,9},{9,8},{10,11... | collective-permute-start | bytes 1572872 | tf_op jit(solution)/shard_map/ppermute | solution.py:63
  193.4 3.4 %copy-start.12 = (f32[8,2,2,32,512]{4,3,2,1,0:T(8,128)S(1)}, f32[8,2,2,32,512]{4,3,2,1,0:T(8,128)}, u32[]{:S(2)}) copy-start(f32[8,2,2,32,512]{4,3,2,1,0:T(8,128)} %copy-done.11) | copy-start | bytes 6291460
  196.5 27.3 %collective-permute-start.11 = (bf16[8,1,32,1536]{3,2,1,0:T(8,128)(2,1)S(1)}, bf16[8,1,32,1536]{3,2,1,0:T(8,128)(2,1)S(1)}, u32[]{:S(2)}, u32[]{:S(2)}) collective-permute-start(bf16[8,1,32,1536]{3,2,1,0:T(8,128)(2,1)S(1)} %dynamic-slice_convert_fusion.1), channel_id=1, source_target_pairs={{0,2},{1,3},{2,0},{3,1},{4,6},{5,7},{6,4},{7,5},{8,10},{9,11},{10,... | collective-permute-start | bytes 2359304 | tf_op jit(solution)/shard_map/ppermute | solution.py:63
  198.0 24.1 %collective-permute-start.16 = (bf16[8,1,32,512]{3,2,1,0:T(8,128)(2,1)S(1)}, bf16[8,1,32,512]{3,2,1,0:T(8,128)(2,1)S(1)}, u32[]{:S(2)}, u32[]{:S(2)}) collective-permute-start(bf16[8,1,32,512]{3,2,1,0:T(8,128)(2,1)S(1)} %dynamic-slice_convert_fusion.3), channel_id=1, source_target_pairs={{0,2},{1,3},{2,0},{3,1},{4,6},{5,7},{6,4},{7,5},{8,10},{9,11},{10,... | collective-permute-start | bytes 786440 | tf_op jit(solution)/shard_map/ppermute | solution.py:63
  222.2 6.4 %collective-permute-start.17 = (bf16[4,32,512]{2,1,0:T(8,128)(2,1)S(1)}, bf16[4,32,512]{2,1,0:T(8,128)(2,1)S(1)}, u32[]{:S(2)}, u32[]{:S(2)}) collective-permute-start(bf16[4,32,512]{2,1,0:T(8,128)(2,1)S(1)} %fusion.69), channel_id=1, source_target_pairs={{0,4},{4,0},{8,12},{12,8},{16,20},{20,16},{24,28},{28,24},{1,5},{5... | collective-permute-start | bytes 393224 | tf_op jit(solution)/shard_map/ppermute | solution.py:63
  224.1 11.8 %collective-permute-start.12 = (bf16[4,32,1536]{2,1,0:T(8,128)(2,1)S(1)}, bf16[4,32,1536]{2,1,0:T(8,128)(2,1)S(1)}, u32[]{:S(2)}, u32[]{:S(2)}) collective-permute-start(bf16[4,32,1536]{2,1,0:T(8,128)(2,1)S(1)} %fusion.48), channel_id=1, source_target_pairs={{0,4},{4,0},{8,12},{12,8},{16,20},{20,16},{24,28},{28,24},{1,5},{5... | collective-permute-start | bytes 1179656 | tf_op jit(solution)/shard_map/ppermute | solution.py:63
  228.7 7.4 %collective-permute-start.18 = (bf16[2,32,512]{2,1,0:T(8,128)(2,1)S(1)}, bf16[2,32,512]{2,1,0:T(8,128)(2,1)S(1)}, u32[]{:S(2)}, u32[]{:S(2)}) collective-permute-start(bf16[2,32,512]{2,1,0:T(8,128)(2,1)S(1)} %fusion.70), channel_id=1, source_target_pairs={{0,8},{4,12},{8,0},{12,4},{16,24},{20,28},{24,16},{28,20},{1,9},{5... | collective-permute-start | bytes 196616 | tf_op jit(solution)/shard_map/ppermute | solution.py:63
  236.0 6.1 %collective-permute-start.13 = (bf16[2,32,1536]{2,1,0:T(8,128)(2,1)S(1)}, bf16[2,32,1536]{2,1,0:T(8,128)(2,1)S(1)}, u32[]{:S(2)}, u32[]{:S(2)}) collective-permute-start(bf16[2,32,1536]{2,1,0:T(8,128)(2,1)S(1)} %fusion.64), channel_id=1, source_target_pairs={{0,8},{4,12},{8,0},{12,4},{16,24},{20,28},{24,16},{28,20},{1,9},{5... | collective-permute-start | bytes 589832 | tf_op jit(solution)/shard_map/ppermute | solution.py:63
  236.1 8.7 %collective-permute-start.19 = (bf16[1,32,512]{2,1,0:T(8,128)(2,1)S(1)}, bf16[1,32,512]{2,1,0:T(8,128)(2,1)S(1)}, u32[]{:S(2)}, u32[]{:S(2)}) collective-permute-start(bf16[1,32,512]{2,1,0:T(8,128)(2,1)S(1)} %dynamic-slice_convert_fusion.7), channel_id=1, source_target_pairs={{0,16},{4,20},{8,24},{12,28},{16,0},{20,4},{24,8},{28,12},{1,17},{... | collective-permute-start | bytes 98312 | tf_op jit(solution)/shard_map/ppermute | solution.py:63
  242.2 5.6 %collective-permute-start.14 = (bf16[1,32,1536]{2,1,0:T(8,128)(2,1)S(1)}, bf16[1,32,1536]{2,1,0:T(8,128)(2,1)S(1)}, u32[]{:S(2)}, u32[]{:S(2)}) collective-permute-start(bf16[1,32,1536]{2,1,0:T(8,128)(2,1)S(1)} %dynamic-slice_convert_fusion.5), channel_id=1, source_target_pairs={{0,16},{4,20},{8,24},{12,28},{16,0},{20,4},{24,8},{28,12},{1,17},{... | collective-permute-start | bytes 294920 | tf_op jit(solution)/shard_map/ppermute | solution.py:63
  (1 other events, 0.8 us)
where the time goes:
time: 251 us; the launch traced here: 248 us
  waiting for transfers between devices  73.1 us (29%)
  local copies, waits for them, and re-layouts  57.8 us (23%)
  starting transfers between devices  46.4 us (18%)
  matrix products  40.9 us (16%)
  other arithmetic  28.9 us (12%)
    ppermute x10, waiting for transfers between devices, halve(): came = lax.ppermute(give, axis_name, stage_perm(count, bit))  32.1 us
    unnamed x79, local copies, waits for them, and re-layouts  28.1 us
    ppermute x6, waiting for transfers between devices, ring_gather(): slots.append(lax.ppermute(slots[-1], 'dp', pairs))  14 us
    ppermute x10, starting transfers between devices, halve(): came = lax.ppermute(give, axis_name, stage_perm(count, bit))  11.6 us
    ppermute x2, waiting for transfers between devices, to_tokens(): lax.ppermute(values[:, received:].astype(jnp.bfloat16), 'dp', partner)  9.45 us
    convert_element_type x4, other arithmetic, ring_reduce(): came = lax.ppermute(total.astype(jnp.bfloat16), 'dp', pairs)  9.36 us
    all_to_all x2, starting transfers between devices, to_experts(): lax.all_to_all(store, 'expert', split_axis=0, concat_axis=2, tiled=True)  8.4 us
    all_to_all x2, starting transfers between devices, to_tokens(): lax.all_to_all(total, 'expert', split_axis=1, concat_axis=0, tiled=True)  8.38 us
  transfers between devices with their start and end apart: 30, of which 13 were waited for; matrix products, arithmetic and copies ran while one was open for 43% of the time, Pallas kernels for 0%

commit v1 on v0

--- a/solution.py
+++ b/solution.py
@@ -139,7 +139,10 @@
         other = lax.ppermute(values[:, received:].astype(jnp.bfloat16), "dp", partner)
         total = (values[:, :received] + other.astype(jnp.float32)).astype(jnp.bfloat16)
         total = total.reshape(local_experts, shards, capacity, width)
-        returned = lax.all_to_all(total, "expert", split_axis=1, concat_axis=0, tiled=True)
+        devices = lax.axis_size("expert")
+        pieces = jnp.stack(jnp.split(total, devices, axis=1), axis=0)
+        pieces = lax.all_to_all(pieces, "expert", split_axis=0, concat_axis=0)
+        returned = jnp.concatenate(pieces, axis=0)
         returned = returned.reshape(all_experts * capacity, width)
         return row_contract(spread, returned)
 

time: 251 us -> 237 us (0.944)
  matrix products: 40.9 us -> 34.7 us
  local copies, waits for them, and re-layouts: 57.8 us -> 52.7 us
  waiting for transfers between devices: 73.1 us -> 69.2 us
    ppermute x2, waiting for transfers between devices: 9.45 us -> 3.82 us  [to_tokens(): lax.ppermute(values[:, received:].astype(jnp.bfloat16), 'dp', partner)]
    unnamed x79 -> x69, local copies, waits for them, and re-layouts: 28.1 us -> 26.4 us
where the time goes in v1:
time: 237 us; the launch traced here: 235 us
  waiting for transfers between devices  69.2 us (29%)
  local copies, waits for them, and re-layouts  52.7 us (22%)
  starting transfers between devices  46.7 us (20%)
  matrix products  34.7 us (15%)
  other arithmetic  30.6 us (13%)
    ppermute x10, waiting for transfers between devices, halve(): came = lax.ppermute(give, axis_name, stage_perm(count, bit))  33.5 us
    unnamed x69, local copies, waits for them, and re-layouts  26.4 us
    ppermute x6, waiting for transfers between devices, ring_gather(): slots.append(lax.ppermute(slots[-1], 'dp', pairs))  16.5 us
    ppermute x10, starting transfers between devices, halve(): came = lax.ppermute(give, axis_name, stage_perm(count, bit))  12.3 us
    convert_element_type x4, other arithmetic, ring_reduce(): came = lax.ppermute(total.astype(jnp.bfloat16), 'dp', pairs)  9.4 us
    all_to_all x2, starting transfers between devices, to_experts(): lax.all_to_all(store, 'expert', split_axis=0, concat_axis=2, tiled=True)  8.42 us
    all_to_all x2, starting transfers between devices, to_tokens(): pieces = lax.all_to_all(pieces, 'expert', split_axis=0, concat_axis=0)  8.39 us
    dot_general x4, matrix products, row_contract(): lax.dot_general(left, right, (((0,), (0,)), ((), ())), preferred_element_...  8.38 us
  transfers between devices with their start and end apart: 30, of which 13 were waited for; matrix products, arithmetic and copies ran while one was open for 43% of the time, Pallas kernels for 0%

profile of v1, /device:TPU:0, one launch (start us, length us, event | category | flops | bytes accessed | tf_op | source)
XLA Modules:
  0.0 235.2 jit_solution(1812069099982817063)
XLA Ops:
  0.6 3.1 %collective-permute-start.1 = (bf16[2,1024,128]{2,1,0:T(8,128)(2,1)}, bf16[2,1024,128]{2,1,0:T(8,128)(2,1)}, u32[]{:S(2)}, u32[]{:S(2)}) collective-permute-start(bf16[2,1024,128]{2,1,0:T(8,128)(2,1)} %param.13), channel_id=1, source_target_pairs={{0,8},{4,12},{8,16},{12,20},{16,24},{20,28},{24,0},{28,4},{1,9},{5... | collective-permute-start | bytes 1572872 | tf_op jit(solution)/shard_map/ppermute | solution.py:96
  3.7 1.6 collective-permute-start.4
  9.0 3.0 %convolution_convert_fusion = bf16[256,1536]{1,0:T(8,128)(2,1)} fusion(bf16[1024,1536]{1,0:T(8,128)(2,1)S(1)} %copy-done, bf16[256,1024]{1,0:T(8,128)(2,1)} %param.8, f32[256]{0:T(256)S(1)} %fusion.71), kind=kOutput, calls=%fused_computation.2 | convolution fusion | flops 806486016 | bytes 4457472 | tf_op jit(solution)/shard_map/dot_general | solution.py:152
  12.0 3.1 %reshape.175 = bf16[2,128,3,8,64]{4,3,2,1,0:T(8,128)(2,1)} reshape(bf16[256,1536]{1,0:T(8,128)(2,1)} %convolution_convert_fusion) | data formatting | bytes 1572864 | tf_op jit(solution)/shard_map/jvp()/reshape | solution.py:40
  15.1 2.5 %fusion.80 = (bf16[2,128,1,8,64]{4,3,2,1,0:T(8,128)(2,1)}, bf16[2,128,1,8,64]{4,3,2,1,0:T(8,128)(2,1)}, bf16[2,128,1,8,64]{4,3,2,1,0:T(8,128)(2,1)}) fusion(bf16[2,128,3,8,64]{4,3,2,1,0:T(8,128)(2,1)} %reshape.175), kind=kLoop, calls=%fused_computation.174 | loop fusion | bytes 1572864 | tf_op jit(solution)/shard_map/jvp()/slice | solution.py:43
  18.9 2.0 copy.105
  20.9 2.0 copy.106
  22.9 1.4 select_reduce_fusion
  29.1 4.2 %all-to-all-start = ((bf16[4,2,48,1024]{3,2,1,0:T(8,128)(2,1)}), bf16[4,2,48,1024]{3,2,1,0:T(8,128)(2,1)}, u32[]{:S(2)}, u32[]{:S(2)}) async-start(bf16[4,2,48,1024]{3,2,1,0:T(8,128)(2,1)} %bitcast.179), calls=%async_computation | async-start | bytes 1572864 | tf_op jit(solution)/shard_map/all_to_all | solution.py:134
  33.3 1.7 collective-permute-start.2
  35.1 2.3 convolution_convert_fusion.1
  38.3 6.8 %all-to-all-done = bf16[4,2,48,1024]{3,2,1,0:T(8,128)(2,1)} async-done(((bf16[4,2,48,1024]{3,2,1,0:T(8,128)(2,1)}), bf16[4,2,48,1024]{3,2,1,0:T(8,128)(2,1)}, u32[]{:S(2)}, u32[]{:S(2)}) %all-to-all-start) | async-done | bytes 786464 | tf_op jit(solution)/shard_map/all_to_all | solution.py:134
  45.0 4.2 %all-to-all-start.2 = ((bf16[4,2,48,1024]{3,2,1,0:T(8,128)(2,1)}), bf16[4,2,48,1024]{3,2,1,0:T(8,128)(2,1)}, u32[]{:S(2)}, u32[]{:S(2)}) async-start(bf16[4,2,48,1024]{3,2,1,0:T(8,128)(2,1)} %bitcast.178), calls=%async_computation.2 | async-start | bytes 1572864 | tf_op jit(solution)/shard_map/all_to_all | solution.py:134
  49.3 2.1 copy.69
  51.4 1.5 collective-permute-start
  52.9 1.6 collective-permute-start.3
  55.3 6.2 %collective-permute-done.5 = bf16[2,128,1024]{2,1,0:T(8,128)(2,1)} collective-permute-done((bf16[2,128,1024]{2,1,0:T(8,128)(2,1)}, bf16[2,128,1024]{2,1,0:T(8,128)(2,1)}, u32[]{:S(2)}, u32[]{:S(2)}) %collective-permute-start.5) | collective-permute-done | bytes 524320 | tf_op jit(solution)/shard_map/ppermute | solution.py:96
  61.5 1.9 constant_dynamic-update-slice_fusion.2
  63.4 1.9 constant_dynamic-update-slice_fusion.6
  66.7 1.6 collective-permute-start.8
  68.2 1.9 constant_dynamic-update-slice_fusion.1
  71.2 1.5 collective-permute-done.3
  72.8 1.9 constant_dynamic-update-slice_fusion
  74.7 8.8 %collective-permute-done.6 = bf16[2,128,1024]{2,1,0:T(8,128)(2,1)} collective-permute-done((bf16[2,128,1024]{2,1,0:T(8,128)(2,1)}, bf16[2,128,1024]{2,1,0:T(8,128)(2,1)}, u32[]{:S(2)}, u32[]{:S(2)}) %collective-permute-start.6) | collective-permute-done | bytes 524320 | tf_op jit(solution)/shard_map/ppermute | solution.py:96
  84.5 3.1 %fusion.40 = f32[2,384,512]{2,1,0:T(8,128)S(1)} fusion(bf16[2,1024,512]{2,1,0:T(8,128)(2,1)} %constant_dynamic-update-slice_fusion, bf16[2,192,1024]{2,1,0:T(8,128)(2,1)} %collective-permute-done, bf16[2,192,1024]{2,1,0:T(8,128)(2,1)} %bitcast.9), kind=kOutput, calls=%fused_computation.92 | convolution fusion | flops 808452096 | bytes 5242880 | tf_op jit(solution)/shard_map/esd,edf->esf/dot_general | solution.py:158
  88.3 1.8 fusion.6
  91.3 1.6 collective-permute-start.9
  93.9 1.6 copy-done.3
  100.7 1.6 collective-permute-start.23
  102.2 2.7 %fusion.39 = f32[2,1024,512]{2,1,0:T(8,128)S(1)} fusion(bf16[2,384,512]{2,1,0:T(8,128)(2,1)S(1)} %fusion.6, bf16[2,192,1024]{2,1,0:T(8,128)(2,1)} %collective-permute-done, bf16[2,192,1024]{2,1,0:T(8,128)(2,1)} %bitcast.9), kind=kOutput, calls=%fused_computation.91 | convolution fusion | flops 808452096 | bytes 6553600 | tf_op jit(solution)/shard_map/esd,esf->edf/dot_general | solution.py:163
  104.9 2.1 copy-done.2
  108.0 3.8 %collective-permute-done.9 = bf16[2,192,1024]{2,1,0:T(8,128)(2,1)S(1)} collective-permute-done((bf16[2,192,1024]{2,1,0:T(8,128)(2,1)S(1)}, bf16[2,192,1024]{2,1,0:T(8,128)(2,1)S(1)}, u32[]{:S(2)}, u32[]{:S(2)}) %collective-permute-start.9) | collective-permute-done | bytes 786464 | tf_op jit(solution)/shard_map/ppermute | solution.py:139
  113.1 4.2 %all-to-all-start.3 = ((bf16[4,2,1,48,1024]{4,3,1,2,0:T(8,128)(2,1)}), bf16[4,2,1,48,1024]{4,3,1,2,0:T(8,128)(2,1)}, u32[]{:S(2)}, u32[]{:S(2)}) async-start(bf16[4,2,1,48,1024]{4,3,1,2,0:T(8,128)(2,1)} %pad_maximum_fusion.9), calls=%async_computation.3 | async-start | bytes 1572864 | tf_op jit(solution)/shard_map/all_to_all | solution.py:144
  117.6 2.5 %fusion.34 = bf16[2,128,1024]{2,1,0:T(8,128)(2,1)} fusion(f32[2,512,1024]{2,1,0:T(8,128)} %copy-done.16, bf16[2,128,1024]{2,1,0:T(8,128)(2,1)} %collective-permute-done.23), kind=kLoop, calls=%fused_computation.78 | loop fusion | flops 786432 | bytes 2097152 | tf_op jit(solution)/shard_map/convert_element_type | solution.py:104
  121.4 7.5 %collective-permute-done.20 = bf16[2,1024,128]{2,1,0:T(8,128)(2,1)} collective-permute-done((bf16[2,1024,128]{2,1,0:T(8,128)(2,1)}, bf16[2,1024,128]{2,1,0:T(8,128)(2,1)}, u32[]{:S(2)}, u32[]{:S(2)}) %collective-permute-start.20) | collective-permute-done | bytes 524320 | tf_op jit(solution)/shard_map/ppermute | solution.py:104
  128.9 2.3 fusion.36
  131.2 2.3 fusion.9
  133.5 2.0 fusion.32
  137.8 1.8 copy.77
  139.6 1.7 reshape.165
  141.3 1.7 fusion.14
  143.0 1.7 fusion.22
  149.9 2.1 copy.84
  151.9 2.3 fusion.42
  154.2 2.7 %copy-done.1 = f32[8,2,2,32,1536]{4,3,2,1,0:T(8,128)} copy-done((f32[8,2,2,32,1536]{4,3,2,1,0:T(8,128)}, f32[8,2,2,32,1536]{4,3,2,1,0:T(8,128)S(1)}, u32[]{:S(2)}) %copy-start.1) | copy-done | bytes 6291480
  159.3 4.2 %all-to-all-start.1 = ((bf16[4,2,1,48,1024]{4,3,1,2,0:T(8,128)(2,1)}), bf16[4,2,1,48,1024]{4,3,1,2,0:T(8,128)(2,1)}, u32[]{:S(2)}, u32[]{:S(2)}) async-start(bf16[4,2,1,48,1024]{4,3,1,2,0:T(8,128)(2,1)} %pad_maximum_fusion.8), calls=%async_computation.1 | async-start | bytes 1572864 | tf_op jit(solution)/shard_map/all_to_all | solution.py:144
  163.5 2.3 fusion.33
  165.9 2.3 fusion.35
  168.2 1.5 collective-permute-start.22
  169.7 2.0 copy.87
  171.7 1.5 fusion.50
  175.4 2.6 %fusion.11 = bf16[256,1024]{1,0:T(8,128)(2,1)} fusion(bf16[384,1024]{1,0:T(8,128)(2,1)} %bitcast.15, bf16[256,1024]{1,0:T(8,128)(2,1)} %copy-done.5, s32[256]{0:T(256)S(1)} %multiply_add_fusion.1), kind=kOutput, calls=%fused_computation.45 | convolution fusion | flops 202211328 | bytes 1836032 | tf_op jit(solution)/shard_map/dot_general | solution.py:24
  178.0 3.0 %bitcast_add_fusion = f32[8,2,32,1536]{3,2,1,0:T(8,128)S(1)} fusion(bf16[8,2,32,1536]{3,2,1,0:T(8,128)(2,1)} %collective-permute-done.10, f32[8,2,2,32,1536]{4,3,2,1,0:T(8,128)} %copy-done.1, s32[]{:T(128)S(6)} %select_n.111), kind=kLoop, calls=%fused_computation | loop fusion | flops 1572864 | bytes 7864324 | tf_op jit(solution)/shard_map/add | solution.py:64
  181.1 2.0 collective-permute-start.11
  184.6 2.5 %slice_add_fusion.2 = f32[2,128,1024]{2,1,0:T(8,128)} fusion(f32[2,512,1024]{2,1,0:T(8,128)} %copy-done.16, bf16[2,128,1024]{2,1,0:T(8,128)(2,1)} %collective-permute-done.25), kind=kLoop, calls=%fused_computation.74 | loop fusion | flops 524288 | bytes 2621440 | tf_op jit(solution)/shard_map/add | solution.py:105
  187.1 19.9 %collective-permute-done.16 = bf16[8,1,32,512]{3,2,1,0:T(8,128)(2,1)S(1)} collective-permute-done((bf16[8,1,32,512]{3,2,1,0:T(8,128)(2,1)S(1)}, bf16[8,1,32,512]{3,2,1,0:T(8,128)(2,1)S(1)}, u32[]{:S(2)}, u32[]{:S(2)}) %collective-permute-start.16) | collective-permute-done | bytes 262176 | tf_op jit(solution)/shard_map/ppermute | solution.py:63
  207.1 1.6 collective-permute-start.17
  209.6 2.4 %slice_add_fusion.5 = f32[2,1024,128]{2,1,0:T(8,128)} fusion(f32[2,1024,512]{2,1,0:T(8,128)} %copy-done.2, bf16[2,1024,128]{2,1,0:T(8,128)(2,1)} %collective-permute-done.22), kind=kLoop, calls=%fused_computation.80 | loop fusion | flops 524288 | bytes 2621440 | tf_op jit(solution)/shard_map/add | solution.py:105
  212.0 1.6 collective-permute-done.17
  213.6 3.4 %collective-permute-start.18 = (bf16[2,32,512]{2,1,0:T(8,128)(2,1)S(1)}, bf16[2,32,512]{2,1,0:T(8,128)(2,1)S(1)}, u32[]{:S(2)}, u32[]{:S(2)}) collective-permute-start(bf16[2,32,512]{2,1,0:T(8,128)(2,1)S(1)} %fusion.70), channel_id=1, source_target_pairs={{0,8},{4,12},{8,0},{12,4},{16,24},{20,28},{24,16},{28,20},{1,9},{5... | collective-permute-start | bytes 196616 | tf_op jit(solution)/shard_map/ppermute | solution.py:63
  217.1 3.8 %collective-permute-done.12 = bf16[4,32,1536]{2,1,0:T(8,128)(2,1)S(1)} collective-permute-done((bf16[4,32,1536]{2,1,0:T(8,128)(2,1)S(1)}, bf16[4,32,1536]{2,1,0:T(8,128)(2,1)S(1)}, u32[]{:S(2)}, u32[]{:S(2)}) %collective-permute-start.12) | collective-permute-done | bytes 393248 | tf_op jit(solution)/shard_map/ppermute | solution.py:63
  221.0 3.4 %collective-permute-start.13 = (bf16[2,32,1536]{2,1,0:T(8,128)(2,1)S(1)}, bf16[2,32,1536]{2,1,0:T(8,128)(2,1)S(1)}, u32[]{:S(2)}, u32[]{:S(2)}) collective-permute-start(bf16[2,32,1536]{2,1,0:T(8,128)(2,1)S(1)} %fusion.64), channel_id=1, source_target_pairs={{0,8},{4,12},{8,0},{12,4},{16,24},{20,28},{24,16},{28,20},{1,9},{5... | collective-permute-start | bytes 589832 | tf_op jit(solution)/shard_map/ppermute | solution.py:63
  224.6 4.3 %collective-permute-done.13 = bf16[2,32,1536]{2,1,0:T(8,128)(2,1)S(1)} collective-permute-done((bf16[2,32,1536]{2,1,0:T(8,128)(2,1)S(1)}, bf16[2,32,1536]{2,1,0:T(8,128)(2,1)S(1)}, u32[]{:S(2)}, u32[]{:S(2)}) %collective-permute-start.13) | collective-permute-done | bytes 196640 | tf_op jit(solution)/shard_map/ppermute | solution.py:63
  230.6 3.9 %collective-permute-done.14 = bf16[1,32,1536]{2,1,0:T(8,128)(2,1)S(1)} collective-permute-done((bf16[1,32,1536]{2,1,0:T(8,128)(2,1)S(1)}, bf16[1,32,1536]{2,1,0:T(8,128)(2,1)S(1)}, u32[]{:S(2)}, u32[]{:S(2)}) %collective-permute-start.14) | collective-permute-done | bytes 98336 | tf_op jit(solution)/shard_map/ppermute | solution.py:63
  (149 shorter events, 44.0 us)
Async XLA Ops:
  0.6 8.4 %copy-start = (bf16[1024,1536]{1,0:T(8,128)(2,1)S(1)}, bf16[1024,1536]{1,0:T(8,128)(2,1)}, u32[]{:S(2)}) copy-start(bf16[1024,1536]{1,0:T(8,128)(2,1)} %param.11) | copy-start | bytes 9437188
  0.6 32.7 %collective-permute-start.1 = (bf16[2,1024,128]{2,1,0:T(8,128)(2,1)}, bf16[2,1024,128]{2,1,0:T(8,128)(2,1)}, u32[]{:S(2)}, u32[]{:S(2)}) collective-permute-start(bf16[2,1024,128]{2,1,0:T(8,128)(2,1)} %param.13), channel_id=1, source_target_pairs={{0,8},{4,12},{8,16},{12,20},{16,24},{20,28},{24,0},{28,4},{1,9},{5... | collective-permute-start | bytes 1572872 | tf_op jit(solution)/shard_map/ppermute | solution.py:96
  3.7 31.3 %collective-permute-start.4 = (bf16[2,128,1024]{2,1,0:T(8,128)(2,1)}, bf16[2,128,1024]{2,1,0:T(8,128)(2,1)}, u32[]{:S(2)}, u32[]{:S(2)}) collective-permute-start(bf16[2,128,1024]{2,1,0:T(8,128)(2,1)} %param.14), channel_id=1, source_target_pairs={{0,8},{4,12},{8,16},{12,20},{16,24},{20,28},{24,0},{28,4},{1,9},{5... | collective-permute-start | bytes 1572872 | tf_op jit(solution)/shard_map/ppermute | solution.py:96
  24.4 1.0 copy-start.12
  24.4 1.4 copy-start.20
  24.4 1.9 copy-start.22
  24.6 1.0 copy-start.11
  25.5 3.5 %copy-start.24 = (bf16[2,128,8,64]{1,0,3,2:T(2,128)(2,1)}, bf16[2,128,8,64]{1,0,3,2:T(2,128)(2,1)S(1)}, u32[]{:S(2)}) copy-start(bf16[2,128,8,64]{1,0,3,2:T(2,128)(2,1)S(1)} %copy.68) | copy-start | bytes 786436
  26.9 0.8 copy-start.5
  29.1 15.9 %all-to-all-start = ((bf16[4,2,48,1024]{3,2,1,0:T(8,128)(2,1)}), bf16[4,2,48,1024]{3,2,1,0:T(8,128)(2,1)}, u32[]{:S(2)}, u32[]{:S(2)}) async-start(bf16[4,2,48,1024]{3,2,1,0:T(8,128)(2,1)} %bitcast.179), calls=%async_computation | async-start | bytes 1572864 | tf_op jit(solution)/shard_map/all_to_all | solution.py:134
  33.3 4.1 %copy-start.26 = (bf16[2,1024,128]{2,1,0:T(8,128)(2,1)S(1)}, bf16[2,1024,128]{2,1,0:T(8,128)(2,1)}, u32[]{:S(2)}) copy-start(bf16[2,1024,128]{2,1,0:T(8,128)(2,1)} %param.13) | copy-start | bytes 1572868
  33.3 19.5 %collective-permute-start.2 = (bf16[2,1024,128]{2,1,0:T(8,128)(2,1)}, bf16[2,1024,128]{2,1,0:T(8,128)(2,1)}, u32[]{:S(2)}, u32[]{:S(2)}) collective-permute-start(bf16[2,1024,128]{2,1,0:T(8,128)(2,1)} %collective-permute-done.1), channel_id=1, source_target_pairs={{0,8},{4,12},{8,16},{12,20},{16,24},{20,28},{24,0},{28,4},{1,9},{5... | collective-permute-start | bytes 1572872 | tf_op jit(solution)/shard_map/ppermute | solution.py:96
  35.0 26.5 %collective-permute-start.5 = (bf16[2,128,1024]{2,1,0:T(8,128)(2,1)}, bf16[2,128,1024]{2,1,0:T(8,128)(2,1)}, u32[]{:S(2)}, u32[]{:S(2)}) collective-permute-start(bf16[2,128,1024]{2,1,0:T(8,128)(2,1)} %collective-permute-done.4), channel_id=1, source_target_pairs={{0,8},{4,12},{8,16},{12,20},{16,24},{20,28},{24,0},{28,4},{1,9},{5... | collective-permute-start | bytes 1572872 | tf_op jit(solution)/shard_map/ppermute | solution.py:96
  45.0 20.3 %all-to-all-start.2 = ((bf16[4,2,48,1024]{3,2,1,0:T(8,128)(2,1)}), bf16[4,2,48,1024]{3,2,1,0:T(8,128)(2,1)}, u32[]{:S(2)}, u32[]{:S(2)}) async-start(bf16[4,2,48,1024]{3,2,1,0:T(8,128)(2,1)} %bitcast.178), calls=%async_computation.2 | async-start | bytes 1572864 | tf_op jit(solution)/shard_map/all_to_all | solution.py:134
  49.2 5.2 %copy-start.27 = (bf16[2,128,1024]{2,1,0:T(8,128)(2,1)S(1)}, bf16[2,128,1024]{2,1,0:T(8,128)(2,1)}, u32[]{:S(2)}) copy-start(bf16[2,128,1024]{2,1,0:T(8,128)(2,1)} %param.14) | copy-start | bytes 1572868
  51.4 33.1 %collective-permute-start = (bf16[2,192,1024]{2,1,0:T(8,128)(2,1)}, bf16[2,192,1024]{2,1,0:T(8,128)(2,1)}, u32[]{:S(2)}, u32[]{:S(2)}) collective-permute-start(bf16[2,192,1024]{2,1,0:T(8,128)(2,1)} %bitcast.9), channel_id=1, source_target_pairs={{0,4},{4,0},{8,12},{12,8},{16,20},{20,16},{24,28},{28,24},{1,5},{5... | collective-permute-start | bytes 2359304 | tf_op jit(solution)/shard_map/ppermute | solution.py:136
  52.9 19.9 %collective-permute-start.3 = (bf16[2,1024,128]{2,1,0:T(8,128)(2,1)}, bf16[2,1024,128]{2,1,0:T(8,128)(2,1)}, u32[]{:S(2)}, u32[]{:S(2)}) collective-permute-start(bf16[2,1024,128]{2,1,0:T(8,128)(2,1)} %collective-permute-done.2), channel_id=1, source_target_pairs={{0,8},{4,12},{8,16},{12,20},{16,24},{20,28},{24,0},{28,4},{1,9},{5... | collective-permute-start | bytes 1572872 | tf_op jit(solution)/shard_map/ppermute | solution.py:96
  61.5 21.9 %collective-permute-start.6 = (bf16[2,128,1024]{2,1,0:T(8,128)(2,1)}, bf16[2,128,1024]{2,1,0:T(8,128)(2,1)}, u32[]{:S(2)}, u32[]{:S(2)}) collective-permute-start(bf16[2,128,1024]{2,1,0:T(8,128)(2,1)} %collective-permute-done.5), channel_id=1, source_target_pairs={{0,8},{4,12},{8,16},{12,20},{16,24},{20,28},{24,0},{28,4},{1,9},{5... | collective-permute-start | bytes 1572872 | tf_op jit(solution)/shard_map/ppermute | solution.py:96
  65.3 4.8 %copy-start.15 = (bf16[2,512,1024]{2,1,0:T(8,128)(2,1)S(1)}, bf16[2,512,1024]{2,1,0:T(8,128)(2,1)}, u32[]{:S(2)}) copy-start(bf16[2,512,1024]{2,1,0:T(8,128)(2,1)} %constant_dynamic-update-slice_fusion.6) | copy-start | bytes 6291460
  66.7 21.7 %collective-permute-start.8 = (bf16[2,192,1024]{2,1,0:T(8,128)(2,1)S(1)}, bf16[2,192,1024]{2,1,0:T(8,128)(2,1)S(1)}, u32[]{:S(2)}, u32[]{:S(2)}) collective-permute-start(bf16[2,192,1024]{2,1,0:T(8,128)(2,1)S(1)} %bitcast.194), channel_id=1, source_target_pairs={{0,4},{4,0},{8,12},{12,8},{16,20},{20,16},{24,28},{28,24},{1,5},{5... | collective-permute-start | bytes 2359304 | tf_op jit(solution)/shard_map/ppermute | solution.py:136
  87.6 2.5 %copy-start.14 = (bf16[2,1024,512]{2,1,0:T(8,128)(2,1)S(1)}, bf16[2,1024,512]{2,1,0:T(8,128)(2,1)}, u32[]{:S(2)}) copy-start(bf16[2,1024,512]{2,1,0:T(8,128)(2,1)} %constant_dynamic-update-slice_fusion) | copy-start | bytes 6291460
  91.3 20.5 %collective-permute-start.9 = (bf16[2,192,1024]{2,1,0:T(8,128)(2,1)S(1)}, bf16[2,192,1024]{2,1,0:T(8,128)(2,1)S(1)}, u32[]{:S(2)}, u32[]{:S(2)}) collective-permute-start(bf16[2,192,1024]{2,1,0:T(8,128)(2,1)S(1)} %slice.45), channel_id=1, source_target_pairs={{0,4},{4,0},{8,12},{12,8},{16,20},{20,16},{24,28},{28,24},{1,5},{5... | collective-permute-start | bytes 2359304 | tf_op jit(solution)/shard_map/ppermute | solution.py:139
  93.9 1.6 copy-start.3
  96.5 34.6 %collective-permute-start.7 = (bf16[2,192,1024]{2,1,0:T(8,128)(2,1)}, bf16[2,192,1024]{2,1,0:T(8,128)(2,1)}, u32[]{:S(2)}, u32[]{:S(2)}) collective-permute-start(bf16[2,192,1024]{2,1,0:T(8,128)(2,1)} %slice.46), channel_id=1, source_target_pairs={{0,4},{4,0},{8,12},{12,8},{16,20},{20,16},{24,28},{28,24},{1,5},{5... | collective-permute-start | bytes 2359304 | tf_op jit(solution)/shard_map/ppermute | solution.py:139
  98.4 2.2 copy-start.16
  100.7 17.0 %collective-permute-start.23 = (bf16[2,128,1024]{2,1,0:T(8,128)(2,1)}, bf16[2,128,1024]{2,1,0:T(8,128)(2,1)}, u32[]{:S(2)}, u32[]{:S(2)}) collective-permute-start(bf16[2,128,1024]{2,1,0:T(8,128)(2,1)} %split.106), channel_id=1, source_target_pairs={{0,8},{4,12},{8,16},{12,20},{16,24},{20,28},{24,0},{28,4},{1,9},{5... | collective-permute-start | bytes 1572872 | tf_op jit(solution)/shard_map/ppermute | solution.py:104
  104.9 2.1 copy-start.2
  107.9 21.0 %collective-permute-start.20 = (bf16[2,1024,128]{2,1,0:T(8,128)(2,1)}, bf16[2,1024,128]{2,1,0:T(8,128)(2,1)}, u32[]{:S(2)}, u32[]{:S(2)}) collective-permute-start(bf16[2,1024,128]{2,1,0:T(8,128)(2,1)} %split.107), channel_id=1, source_target_pairs={{0,8},{4,12},{8,16},{12,20},{16,24},{20,28},{24,0},{28,4},{1,9},{5... | collective-permute-start | bytes 1572872 | tf_op jit(solution)/shard_map/ppermute | solution.py:104
  113.1 20.4 %all-to-all-start.3 = ((bf16[4,2,1,48,1024]{4,3,1,2,0:T(8,128)(2,1)}), bf16[4,2,1,48,1024]{4,3,1,2,0:T(8,128)(2,1)}, u32[]{:S(2)}, u32[]{:S(2)}) async-start(bf16[4,2,1,48,1024]{4,3,1,2,0:T(8,128)(2,1)} %pad_maximum_fusion.9), calls=%async_computation.3 | async-start | bytes 1572864 | tf_op jit(solution)/shard_map/all_to_all | solution.py:144
  117.6 13.5 %copy-start.4 = (f32[2,384,1024]{2,1,0:T(8,128)S(1)}, f32[2,384,1024]{2,1,0:T(8,128)}, u32[]{:S(2)}) copy-start(f32[2,384,1024]{2,1,0:T(8,128)} %copy-done.3) | copy-start | bytes 9437188
  120.1 43.4 %collective-permute-start.24 = (bf16[2,128,1024]{2,1,0:T(8,128)(2,1)}, bf16[2,128,1024]{2,1,0:T(8,128)(2,1)}, u32[]{:S(2)}, u32[]{:S(2)}) collective-permute-start(bf16[2,128,1024]{2,1,0:T(8,128)(2,1)} %fusion.34), channel_id=1, source_target_pairs={{0,8},{4,12},{8,16},{12,20},{16,24},{20,28},{24,0},{28,4},{1,9},{5... | collective-permute-start | bytes 1572872 | tf_op jit(solution)/shard_map/ppermute | solution.py:104
  131.2 34.7 %collective-permute-start.21 = (bf16[2,1024,128]{2,1,0:T(8,128)(2,1)}, bf16[2,1024,128]{2,1,0:T(8,128)(2,1)}, u32[]{:S(2)}, u32[]{:S(2)}) collective-permute-start(bf16[2,1024,128]{2,1,0:T(8,128)(2,1)} %fusion.36), channel_id=1, source_target_pairs={{0,8},{4,12},{8,16},{12,20},{16,24},{20,28},{24,0},{28,4},{1,9},{5... | collective-permute-start | bytes 1572872 | tf_op jit(solution)/shard_map/ppermute | solution.py:104
  133.5 2.0 copy-start.6
  133.5 2.0 copy-start.19
  133.5 3.2 %copy-start.23 = (bf16[1024,512]{1,0:T(8,128)(2,1)S(1)}, bf16[1024,512]{1,0:T(8,128)(2,1)}, u32[]{:S(2)}) copy-start(bf16[1024,512]{1,0:T(8,128)(2,1)} %param.12) | copy-start | bytes 3145732
  135.9 0.8 copy-start.7
  141.3 3.4 %copy-start.13 = (f32[2,8,128,128]{2,3,1,0:T(8,128)S(1)}, f32[2,8,128,128]{2,3,1,0:T(8,128)}, u32[]{:S(2)}) copy-start(f32[2,8,128,128]{2,3,1,0:T(8,128)} %copy-done.12) | copy-start | bytes 3145732
  141.3 3.4 %copy-start.29 = (bf16[2,128,1,8,64]{1,4,3,0,2:T(8,128)(2,1)S(1)}, bf16[2,128,1,8,64]{1,4,3,0,2:T(8,128)(2,1)}, u32[]{:S(2)}) copy-start(bf16[2,128,1,8,64]{1,4,3,0,2:T(8,128)(2,1)} %copy.106) | copy-start | bytes 786436
  144.8 1.0 copy-start.28
  146.2 1.1 copy-start.21
  147.1 1.3 copy-start.17
  147.3 1.2 copy-start.8
  154.2 2.7 %copy-start.1 = (f32[8,2,2,32,1536]{4,3,2,1,0:T(8,128)}, f32[8,2,2,32,1536]{4,3,2,1,0:T(8,128)S(1)}, u32[]{:S(2)}) copy-start(f32[8,2,2,32,1536]{4,3,2,1,0:T(8,128)S(1)} %fusion.42) | copy-start | bytes 18874372
  156.9 1.4 copy-start.18
  158.3 19.8 %collective-permute-start.10 = (bf16[8,2,32,1536]{3,2,1,0:T(8,128)(2,1)}, bf16[8,2,32,1536]{3,2,1,0:T(8,128)(2,1)}, u32[]{:S(2)}, u32[]{:S(2)}) collective-permute-start(bf16[8,2,32,1536]{3,2,1,0:T(8,128)(2,1)} %fusion.7), channel_id=1, source_target_pairs={{0,1},{1,0},{2,3},{3,2},{4,5},{5,4},{6,7},{7,6},{8,9},{9,8},{10,11... | collective-permute-start | bytes 4718600 | tf_op jit(solution)/shard_map/ppermute | solution.py:63
  159.3 16.1 %all-to-all-start.1 = ((bf16[4,2,1,48,1024]{4,3,1,2,0:T(8,128)(2,1)}), bf16[4,2,1,48,1024]{4,3,1,2,0:T(8,128)(2,1)}, u32[]{:S(2)}, u32[]{:S(2)}) async-start(bf16[4,2,1,48,1024]{4,3,1,2,0:T(8,128)(2,1)} %pad_maximum_fusion.8), calls=%async_computation.1 | async-start | bytes 1572864 | tf_op jit(solution)/shard_map/all_to_all | solution.py:144
  165.8 5.9 %copy-start.25 = (bf16[2,128,8,64]{1,0,3,2:T(2,128)(2,1)S(1)}, bf16[2,128,8,64]{1,0,3,2:T(2,128)(2,1)}, u32[]{:S(2)}) copy-start(bf16[2,128,8,64]{1,0,3,2:T(2,128)(2,1)} %copy-done.24) | copy-start | bytes 786436
  165.8 18.7 %collective-permute-start.25 = (bf16[2,128,1024]{2,1,0:T(8,128)(2,1)}, bf16[2,128,1024]{2,1,0:T(8,128)(2,1)}, u32[]{:S(2)}, u32[]{:S(2)}) collective-permute-start(bf16[2,128,1024]{2,1,0:T(8,128)(2,1)} %fusion.33), channel_id=1, source_target_pairs={{0,8},{4,12},{8,16},{12,20},{16,24},{20,28},{24,0},{28,4},{1,9},{5... | collective-permute-start | bytes 1572872 | tf_op jit(solution)/shard_map/ppermute | solution.py:104
  168.2 41.4 %collective-permute-start.22 = (bf16[2,1024,128]{2,1,0:T(8,128)(2,1)}, bf16[2,1024,128]{2,1,0:T(8,128)(2,1)}, u32[]{:S(2)}, u32[]{:S(2)}) collective-permute-start(bf16[2,1024,128]{2,1,0:T(8,128)(2,1)} %fusion.35), channel_id=1, source_target_pairs={{0,8},{4,12},{8,16},{12,20},{16,24},{20,28},{24,0},{28,4},{1,9},{5... | collective-permute-start | bytes 1572872 | tf_op jit(solution)/shard_map/ppermute | solution.py:104
  173.3 1.3 copy-start.9
  175.4 7.7 %collective-permute-start.15 = (bf16[8,2,32,512]{3,2,1,0:T(8,128)(2,1)}, bf16[8,2,32,512]{3,2,1,0:T(8,128)(2,1)}, u32[]{:S(2)}, u32[]{:S(2)}) collective-permute-start(bf16[8,2,32,512]{3,2,1,0:T(8,128)(2,1)} %fusion.45), channel_id=1, source_target_pairs={{0,1},{1,0},{2,3},{3,2},{4,5},{5,4},{6,7},{7,6},{8,9},{9,8},{10,11... | collective-permute-start | bytes 1572872 | tf_op jit(solution)/shard_map/ppermute | solution.py:63
  178.0 5.2 %copy-start.10 = (f32[8,2,2,32,512]{4,3,2,1,0:T(8,128)S(1)}, f32[8,2,2,32,512]{4,3,2,1,0:T(8,128)}, u32[]{:S(2)}) copy-start(f32[8,2,2,32,512]{4,3,2,1,0:T(8,128)} %copy-done.9) | copy-start | bytes 6291460
  181.1 27.5 %collective-permute-start.11 = (bf16[8,1,32,1536]{3,2,1,0:T(8,128)(2,1)S(1)}, bf16[8,1,32,1536]{3,2,1,0:T(8,128)(2,1)S(1)}, u32[]{:S(2)}, u32[]{:S(2)}) collective-permute-start(bf16[8,1,32,1536]{3,2,1,0:T(8,128)(2,1)S(1)} %dynamic-slice_convert_fusion.1), channel_id=1, source_target_pairs={{0,2},{1,3},{2,0},{3,1},{4,6},{5,7},{6,4},{7,5},{8,10},{9,11},{10,... | collective-permute-start | bytes 2359304 | tf_op jit(solution)/shard_map/ppermute | solution.py:63
  184.5 22.6 %collective-permute-start.16 = (bf16[8,1,32,512]{3,2,1,0:T(8,128)(2,1)S(1)}, bf16[8,1,32,512]{3,2,1,0:T(8,128)(2,1)S(1)}, u32[]{:S(2)}, u32[]{:S(2)}) collective-permute-start(bf16[8,1,32,512]{3,2,1,0:T(8,128)(2,1)S(1)} %dynamic-slice_convert_fusion.3), channel_id=1, source_target_pairs={{0,2},{1,3},{2,0},{3,1},{4,6},{5,7},{6,4},{7,5},{8,10},{9,11},{10,... | collective-permute-start | bytes 786440 | tf_op jit(solution)/shard_map/ppermute | solution.py:63
  207.1 6.4 %collective-permute-start.17 = (bf16[4,32,512]{2,1,0:T(8,128)(2,1)S(1)}, bf16[4,32,512]{2,1,0:T(8,128)(2,1)S(1)}, u32[]{:S(2)}, u32[]{:S(2)}) collective-permute-start(bf16[4,32,512]{2,1,0:T(8,128)(2,1)S(1)} %fusion.69), channel_id=1, source_target_pairs={{0,4},{4,0},{8,12},{12,8},{16,20},{20,16},{24,28},{28,24},{1,5},{5... | collective-permute-start | bytes 393224 | tf_op jit(solution)/shard_map/ppermute | solution.py:63
  209.0 11.9 %collective-permute-start.12 = (bf16[4,32,1536]{2,1,0:T(8,128)(2,1)S(1)}, bf16[4,32,1536]{2,1,0:T(8,128)(2,1)S(1)}, u32[]{:S(2)}, u32[]{:S(2)}) collective-permute-start(bf16[4,32,1536]{2,1,0:T(8,128)(2,1)S(1)} %fusion.48), channel_id=1, source_target_pairs={{0,4},{4,0},{8,12},{12,8},{16,20},{20,16},{24,28},{28,24},{1,5},{5... | collective-permute-start | bytes 1179656 | tf_op jit(solution)/shard_map/ppermute | solution.py:63
  213.6 10.8 %collective-permute-start.18 = (bf16[2,32,512]{2,1,0:T(8,128)(2,1)S(1)}, bf16[2,32,512]{2,1,0:T(8,128)(2,1)S(1)}, u32[]{:S(2)}, u32[]{:S(2)}) collective-permute-start(bf16[2,32,512]{2,1,0:T(8,128)(2,1)S(1)} %fusion.70), channel_id=1, source_target_pairs={{0,8},{4,12},{8,0},{12,4},{16,24},{20,28},{24,16},{28,20},{1,9},{5... | collective-permute-start | bytes 196616 | tf_op jit(solution)/shard_map/ppermute | solution.py:63
  221.0 7.9 %collective-permute-start.13 = (bf16[2,32,1536]{2,1,0:T(8,128)(2,1)S(1)}, bf16[2,32,1536]{2,1,0:T(8,128)(2,1)S(1)}, u32[]{:S(2)}, u32[]{:S(2)}) collective-permute-start(bf16[2,32,1536]{2,1,0:T(8,128)(2,1)S(1)} %fusion.64), channel_id=1, source_target_pairs={{0,8},{4,12},{8,0},{12,4},{16,24},{20,28},{24,16},{28,20},{1,9},{5... | collective-permute-start | bytes 589832 | tf_op jit(solution)/shard_map/ppermute | solution.py:63
  224.5 5.5 %collective-permute-start.19 = (bf16[1,32,512]{2,1,0:T(8,128)(2,1)S(1)}, bf16[1,32,512]{2,1,0:T(8,128)(2,1)S(1)}, u32[]{:S(2)}, u32[]{:S(2)}) collective-permute-start(bf16[1,32,512]{2,1,0:T(8,128)(2,1)S(1)} %dynamic-slice_convert_fusion.7), channel_id=1, source_target_pairs={{0,16},{4,20},{8,24},{12,28},{16,0},{20,4},{24,8},{28,12},{1,17},{... | collective-permute-start | bytes 98312 | tf_op jit(solution)/shard_map/ppermute | solution.py:63
  229.0 5.6 %collective-permute-start.14 = (bf16[1,32,1536]{2,1,0:T(8,128)(2,1)S(1)}, bf16[1,32,1536]{2,1,0:T(8,128)(2,1)S(1)}, u32[]{:S(2)}, u32[]{:S(2)}) collective-permute-start(bf16[1,32,1536]{2,1,0:T(8,128)(2,1)S(1)} %dynamic-slice_convert_fusion.5), channel_id=1, source_target_pairs={{0,16},{4,20},{8,24},{12,28},{16,0},{20,4},{24,8},{28,12},{1,17},{... | collective-permute-start | bytes 294920 | tf_op jit(solution)/shard_map/ppermute | solution.py:63
